TPU v7x, 256 devices: a whole 4x4x8 slice. The times are simulated.
256 devices in a mesh: grp: 2 (over z_lo), gx: 32 (over x, y, core), gy: 4 (over z_hi).
Axes of the slice: x: 4, y: 4, z: 8 (z_hi: 4, z_lo: 2; z = z_hi * 2 + z_lo), core: 2. Of those that a mesh axis runs over, the one named last changes fastest.
Arguments:
- velocity: float32 [3, 256, 128, 256], P(None, 'gx', 'gy', 'grp'), may hold values from -6 to 6
- viscosity: float32 [256, 128, 256], P('gx', 'gy', 'grp'), may hold values from 0.02 to 0.15
- selection: int32 [2, 32, 4, 96], P('grp', 'gx', 'gy'), may hold values from 0 to 255
- w_in: bfloat16 [384, 1024], replicated, may hold values from -0.3125 to 0.3125
- w_up: bfloat16 [1024, 4096], P(None, 'gy'), may hold values from -0.1875 to 0.1875
- w_down: bfloat16 [4096, 1024], P('gy'), may hold values from -0.09375 to 0.09375
- w_out: bfloat16 [1024, 384], replicated, may hold values from -0.1875 to 0.1875
Outputs:
- velocity_next: float32 [3, 256, 128, 256], P(None, 'gx', 'gy', 'grp')
- pressure: float32 [256, 128, 256], P('gx', 'gy', 'grp')
- grad_in: float32 [384, 1024], P(None, ('grp', 'gx', 'gy'))
- grad_up: float32 [1024, 4096], P(('grp', 'gx'), 'gy')
- grad_down: float32 [4096, 1024], P('gy', ('grp', 'gx'))
- grad_out: float32 [1024, 384], P(('grp', 'gx', 'gy'))
Inputs may be any that keep to these rules, and one draw needn't show every extreme that they name: `selection`: each entry numbers a patch of the device's own block.
All inputs are finite; a program needn't handle non-finite values.
Results may differ from a plain program's by a relative error of at most 0.0055.
Values may be sent and summed in bfloat16 or wider, within the bound.
A program may use at most 128 MiB of HBM per device.

v0:
```python
import jax
import jax.numpy as jnp
from jax import lax
from jax.experimental import pallas as pl
from jax.experimental.pallas import tpu as pltpu
from jax.sharding import PartitionSpec as P

F32 = jnp.float32
BF16 = jnp.bfloat16
MESH = pl.DeviceIdType.MESH
MIB = 1 << 20

FACES = [(1, 0), (-1, 0), (0, 1), (0, -1)]
DIAGONALS = [(1, 1), (1, -1), (-1, 1), (-1, -1)]
PLANE = FACES + DIAGONALS
CROSS_ONE = [(0, 0)] + FACES
CROSS_TWO = [(0, 0)] + PLANE


def place():
    return lax.axis_index("grp"), lax.axis_index("gx"), lax.axis_index("gy")


def push(src, dst, sems, slot, target):
    return pltpu.make_async_remote_copy(
        src_ref=src,
        dst_ref=dst,
        send_sem=sems.at[0, slot],
        recv_sem=sems.at[1, slot],
        device_id=target,
        device_id_type=MESH,
    )


def greet(targets):
    barrier = pltpu.get_barrier_semaphore()
    for target in targets:
        pl.semaphore_signal(barrier, inc=1, device_id=target, device_id_type=MESH)


def greeted(targets):
    pl.semaphore_wait(pltpu.get_barrier_semaphore(), len(targets))


def matmul(a, b):
    return jnp.dot(a, b, preferred_element_type=F32)


def matmul_nt(a, b):
    return lax.dot_general(a, b, (((1,), (1,)), ((), ())), preferred_element_type=F32)


def matmul_tn(a, b):
    return lax.dot_general(a, b, (((0,), (0,)), ((), ())), preferred_element_type=F32)


def iota(shape, dim):
    return lax.broadcasted_iota(jnp.int32, shape, dim)


def offset(here, dx, dy, flip):
    g, i, k = here
    return (1 - g if flip else g, lax.rem(i + dx + 32, 32), lax.rem(k + dy + 4, 4))


def stencil_targets(here):
    return [offset(here, dx, dy, False) for dx, dy in PLANE] + [
        offset(here, dx, dy, True) for dx, dy in CROSS_TWO
    ]


def pack_edge(g, group):
    lane = iota((16, 128), 1) // 8
    packed = jnp.zeros((16, 128), F32)
    for part in range(16):
        moved = pltpu.roll(group(part), lax.rem(8 * part + 8 * (1 - g), 128), 1)
        packed = jnp.where(lane == part, moved, packed)
    return packed


def unpack_edge(g, packed, part):
    lane = iota((16, 128), 1)
    rows = pltpu.roll(packed, lax.rem(128 - 8 * part + 120 * g, 128), 1)
    return jnp.where((lane - 120 * g) >> 3 == 0, rows, 0.0)


def unpack_block(g, packed, dx, dy, deep, store):
    planes = range(8) if dx == 0 else (range(8 - deep, 8) if dx < 0 else range(deep))
    for x in planes:
        to = deep + x if dx == 0 else (x - (8 - deep) if dx < 0 else deep + 8 + x)
        if dy == 0:
            store(to, 8, unpack_edge(g, packed, 2 * x))
            store(to, 24, unpack_edge(g, packed, 2 * x + 1))
        elif dy < 0:
            store(to, 0, unpack_edge(g, packed, 2 * x + 1)[8:16])
        else:
            store(to, 40, unpack_edge(g, packed, 2 * x)[0:8])


def along_z(own, other):
    lane = iota(own.shape, 1)
    own_r, other_r = pltpu.roll(own, 127, 1), pltpu.roll(other, 127, 1)
    own_l, other_l = pltpu.roll(own, 1, 1), pltpu.roll(other, 1, 1)
    last, first = lane == 127, lane == 0
    right = (jnp.where(last, other_r, own_r), jnp.where(last, own_r, other_r))
    left = (jnp.where(first, other_l, own_l), jnp.where(first, own_l, other_l))
    return right, left


def own_slices(dx, dy, deep, rows):
    xs = slice(0, 8) if dx == 0 else (slice(8 - deep, 8) if dx > 0 else slice(0, deep))
    ys = slice(0, 32) if dy == 0 else (slice(32 - rows, 32) if dy > 0 else slice(0, rows))
    return xs, ys


class Stencil:
    scratch = [
        pltpu.VMEM((4, 8, 32, 128), F32),
        pltpu.VMEM((2, 4, 8, 2, 128), F32),
        pltpu.VMEM((2, 4, 8, 2, 128), F32),
        pltpu.VMEM((4, 4, 2, 2, 128), F32),
        pltpu.VMEM((4, 16, 128), F32),
        pltpu.VMEM((5, 4, 16, 128), F32),
        pltpu.VMEM((4, 2, 12, 48, 128), F32),
        pltpu.VMEM((3, 2, 12, 48, 128), F32),
        pltpu.VMEM((8, 32, 128), F32),
        pltpu.VMEM((16, 128), F32),
        pltpu.VMEM((9, 16, 128), F32),
        pltpu.VMEM((2, 20, 48, 128), F32),
        pltpu.VMEM((2, 20, 64, 128), F32),
        pltpu.VMEM((2, 20, 64, 128), F32),
        pltpu.SemaphoreType.DMA((2, 13)),
        pltpu.SemaphoreType.DMA((2, 17)),
    ]

    def __init__(self, here, velocity_next, pressure, refs):
        self.here = here
        self.velocity_next, self.pressure = velocity_next, pressure
        (
            self.fields, self.y_send, self.y_recv, self.d_recv, self.z_send, self.z_recv,
            self.wide, self.prov, self.source, self.sz_send, self.sz_recv, self.swide,
            self.p_a, self.p_b, self.sems_one, self.sems_two,
        ) = refs

    def prepare(self):
        g = self.here[0]
        self.y_send[0] = self.fields[:, :, 30:32, :]
        self.y_send[1] = self.fields[:, :, 0:2, :]
        for f in range(4):
            self.z_send[f] = pack_edge(
                g, lambda part: self.fields[f, part // 2, 16 * (part % 2) : 16 * (part % 2) + 16, :]
            )

    def send_one(self):
        g = self.here[0]
        copies = []
        for dx, dy in PLANE:
            slot = len(copies)
            target = offset(self.here, dx, dy, False)
            xs, _ = own_slices(dx, dy, 2, 2)
            if dy == 0:
                x_to = 0 if dx > 0 else 10
                src = self.fields.at[:, xs]
                dst = self.wide.at[:, 0, x_to : x_to + 2, 8:40, :]
            elif dx == 0:
                edge = 0 if dy > 0 else 1
                src, dst = self.y_send.at[edge], self.y_recv.at[edge]
            else:
                edge = 0 if dy > 0 else 1
                src, dst = self.y_send.at[edge, :, xs], self.d_recv.at[slot - 4]
            copies.append(push(src, dst, self.sems_one, slot, target))
        for n, (dx, dy) in enumerate(CROSS_ONE):
            target = offset(self.here, dx, dy, True)
            copies.append(push(self.z_send, self.z_recv.at[n], self.sems_one, len(copies), target))
        for copy in copies:
            copy.start()
        self.copies_one = copies

    def make_source(self):
        g, i, k = self.here
        wide = self.wide
        wide[:, 0, 2:10, 8:40, :] = self.fields[...]
        for copy in self.copies_one:
            copy.wait_recv()
        wide[:, 0, 2:10, 6:8, :] = self.y_recv[0]
        wide[:, 0, 2:10, 40:42, :] = self.y_recv[1]
        for n, (dx, dy) in enumerate(DIAGONALS):
            x_to, y_to = (0 if dx > 0 else 10), (6 if dy > 0 else 40)
            wide[:, 0, x_to : x_to + 2, y_to : y_to + 2, :] = self.d_recv[n]
        for n, (dx, dy) in enumerate(CROSS_ONE):
            for f in (0, 1, 2, 3) if n == 0 else ((0, 2) if dx else (1, 2)):

                def store(to, row, rows, f=f):
                    wide[f, 1, to, row : row + rows.shape[0], :] = rows

                unpack_block(g, self.z_recv[n, f], -dx, -dy, 2, store)

        @pl.when(i == 0)
        def _():
            wide[:, :, 0:2] = jnp.zeros((4, 2, 2, 48, 128), F32)

        @pl.when(i == 31)
        def _():
            wide[:, :, 10:12] = jnp.zeros((4, 2, 2, 48, 128), F32)

        @pl.when(k == 0)
        def _():
            wide[:, :, :, 0:8, :] = jnp.zeros((4, 2, 12, 8, 128), F32)

        @pl.when(k == 3)
        def _():
            wide[:, :, :, 40:48, :] = jnp.zeros((4, 2, 12, 8, 128), F32)

        def advance(c, x, top, bottom, tiles):
            mid = [wide[c, t, x, top:bottom, :] for t in range(2)]
            right, left = along_z(*mid)
            for t in tiles:
                total = wide[c, t, x + 1, top:bottom, :] + wide[c, t, x - 1, top:bottom, :]
                total = total + wide[c, t, x, top + 1 : bottom + 1, :]
                total = total + wide[c, t, x, top - 1 : bottom - 1, :]
                total = total + right[t] + left[t]
                after = mid[t] + wide[3, t, x, top:bottom, :] * (total - 6.0 * mid[t])
                self.prov[c, t, x, top:bottom, :] = after

        def provisional(x, carry):
            advance(0, x, 8, 40, (0,))
            advance(1, x, 7, 41, (0,))
            advance(2, x, 8, 40, (0, 1))
            return carry

        advance(0, 1, 8, 40, (0,))
        advance(0, 10, 8, 40, (0,))
        lax.fori_loop(2, 10, provisional, 0)
        prov = self.prov

        def source(x, carry):
            right, left = along_z(prov[2, 0, x, 8:40, :], prov[2, 1, x, 8:40, :])
            slope = right[0] - left[0]
            slope = slope + prov[0, 0, x + 1, 8:40, :] - prov[0, 0, x - 1, 8:40, :]
            slope = slope + prov[1, 0, x, 9:41, :] - prov[1, 0, x, 7:39, :]
            self.source[x - 2] = 0.5 * slope
            return carry

        lax.fori_loop(2, 10, source, 0)
        self.sz_send[...] = pack_edge(
            g, lambda part: self.source[part // 2, 16 * (part % 2) : 16 * (part % 2) + 16, :]
        )

    def send_two(self):
        g = self.here[0]
        copies = []
        for dx, dy in PLANE:
            target = offset(self.here, dx, dy, False)
            xs, ys = own_slices(dx, dy, 6, 8)
            x_to = 6 if dx == 0 else (0 if dx > 0 else 14)
            y_to = 8 if dy == 0 else (0 if dy > 0 else 40)
            dst = self.swide.at[
                0, x_to : x_to + xs.stop - xs.start, y_to : y_to + ys.stop - ys.start, :
            ]
            copies.append(push(self.source.at[xs, ys, :], dst, self.sems_two, len(copies), target))
        for n, (dx, dy) in enumerate(CROSS_TWO):
            target = offset(self.here, dx, dy, True)
            copies.append(push(self.sz_send, self.sz_recv.at[n], self.sems_two, len(copies), target))
        for copy in copies:
            copy.start()
        self.copies_two = copies

    def solve(self):
        g, i, k = self.here
        swide = self.swide
        swide[0, 6:14, 8:40, :] = self.source[...]
        for copy in self.copies_two:
            copy.wait_recv()
        for n, (dx, dy) in enumerate(CROSS_TWO):

            def store(to, row, rows):
                swide[1, to, row : row + rows.shape[0], :] = rows

            unpack_block(g, self.sz_recv[n], -dx, -dy, 6, store)
        row, lane = iota((48, 128), 0), iota((48, 128), 1)
        outside = ((k == 0) & (row < 8)) | ((k == 3) & (row >= 40))
        sixth = jnp.where(outside, 0.0, 1.0 / 6.0).astype(F32)
        sixths = (sixth, jnp.where((lane - 120 * g) >> 3 == 0, sixth, 0.0))

        def inside(x):
            out = ((i == 0) & (x < 6)) | ((i == 31) & (x >= 14))
            scale = jnp.where(out, 0.0, 1.0).astype(F32)
            return [one * scale for one in sixths]

        def first(x, carry):
            scale = inside(x)
            for t in range(2):
                self.p_a[t, x, 8:56, :] = -swide[t, x] * scale[t]
            return carry

        lax.fori_loop(0, 20, first, 0)
        old, new = self.p_a, self.p_b
        for sweep in range(1, 6):

            def relax(x, carry, old=old, new=new):
                scale = inside(x)
                right, left = along_z(old[0, x, 8:56, :], old[1, x, 8:56, :])
                for t in range(2):
                    total = old[t, x + 1, 8:56, :] + old[t, x - 1, 8:56, :]
                    total = total + old[t, x, 9:57, :] + old[t, x, 7:55, :]
                    total = total + right[t] + left[t]
                    new[t, x, 8:56, :] = (total - swide[t, x]) * scale[t]
                return carry

            lax.fori_loop(sweep, 20 - sweep, relax, 0)
            old, new = new, old
        p, prov = old, self.prov

        def project(x, carry):
            at = x + 6
            right, left = along_z(p[0, at, 16:48, :], p[1, at, 16:48, :])
            slope_z = right[0] - left[0]
            slope_x = p[0, at + 1, 16:48, :] - p[0, at - 1, 16:48, :]
            slope_y = p[0, at, 17:49, :] - p[0, at, 15:47, :]
            for c, slope in enumerate((slope_x, slope_y, slope_z)):
                self.velocity_next[c, x] = prov[c, 0, x + 2, 8:40, :] - 0.5 * slope
            self.pressure[x] = p[0, at, 16:48, :]
            return carry

        lax.fori_loop(0, 8, project, 0)

    def finish(self):
        for copy in self.copies_one + self.copies_two:
            copy.wait_send()


PATCH_SCRATCH = [pltpu.VMEM((16, 6144), F32), pltpu.VMEM((2048, 128), BF16)]


def make_fold(fold):
    row, col = iota((2048, 128), 0), iota((2048, 128), 1)
    hit = (row // 128 == col // 8) & (row % 8 == col % 8)
    fold[...] = hit.astype(F32).astype(BF16)


def pick_patches(field, selection, lines, fold, out):
    for c in range(3):
        for x in range(8):
            for py in range(4):
                combo = (c * 4 + x % 4) * 4 + py
                row = 8 * (x // 4)
                lines[row : row + 8, 128 * combo : 128 * combo + 128] = field[
                    c, x, pl.ds(py, 8, stride=4), :
                ]
    chosen = jnp.broadcast_to(selection[...], (16, 96))
    line = (chosen >> 4 == iota((16, 96), 0)).astype(F32).astype(BF16)
    cell = (chosen & 15 == iota((16, 96), 0)).astype(F32).astype(BF16)
    spread = ((iota((16, 2048), 1) & 127) >> 3 == iota((16, 2048), 0)).astype(F32).astype(BF16)
    here = matmul_tn(cell, spread)
    for part in range(3):
        source = lines[:, 2048 * part : 2048 * part + 2048].astype(BF16)
        rows = (matmul_tn(line, source) * here).astype(BF16)
        out[:, 128 * part : 128 * part + 128] = matmul(rows, fold[...]).astype(BF16)


def trainer_targets(here):
    g, i, k = here
    x, y, c = lax.div(i, 8), lax.rem(lax.div(i, 2), 4), lax.rem(i, 2)
    out = [(g, i, lax.rem(k + d, 4)) for d in (1, 2, 3)]
    out += [(g, lax.rem(x + d, 4) * 8 + y * 2 + c, k) for d in (1, 2, 3)]
    out += [(g, x * 8 + lax.rem(y + d, 4) * 2 + c, k) for d in (1, 2, 3)]
    return out + [(g, x * 8 + y * 2 + 1 - c, k), (1 - g, i, k)]


class Scatter:
    @staticmethod
    def scratch(rows, width, wire):
        return [
            pltpu.VMEM((2, 4, 4, 2, rows, width), F32),
            pltpu.VMEM((2, 4, 4, rows, width), F32),
            pltpu.VMEM((4, 2, 4, rows, width), wire),
            pltpu.VMEM((4, 2, 4, rows, width), wire),
            pltpu.VMEM((2, 4, rows, width), F32),
            pltpu.VMEM((4, 2, rows, width), F32),
            pltpu.VMEM((2, rows, width), F32),
            pltpu.VMEM((rows, width), F32),
            pltpu.SemaphoreType.DMA((2, 8)),
            pltpu.SemaphoreType.DMA((2, 4)),
            pltpu.SemaphoreType.DMA((2, 4)),
            pltpu.SemaphoreType.DMA((2, 1)),
        ]

    def __init__(self, here, refs, wire, x_first):
        g, i, k = here
        self.here, self.wire, self.x_first = here, wire, x_first
        self.x, self.y, self.c = lax.div(i, 8), lax.rem(lax.div(i, 2), 4), lax.rem(i, 2)
        (
            self.parts, self.core_recv, self.one_send, self.one_recv, self.one_sum,
            self.two_recv, self.two_sum, self.three_recv,
            self.core_sems, self.one_sems, self.two_sems, self.three_sems,
        ) = refs

    def along(self, on_x, d):
        g, i, k = self.here
        x, y = self.x, self.y
        if on_x:
            x = lax.rem(x + d, 4)
        else:
            y = lax.rem(y + d, 4)
        return (g, x * 8 + y * 2 + self.c, k)

    def core_copy(self, chunk):
        g, i, k = self.here
        half, x = lax.div(chunk, 4), lax.rem(chunk, 4)
        return push(
            self.parts.at[half, x, :, 1 - self.c],
            self.core_recv.at[half, x],
            self.core_sems,
            chunk,
            (g, self.x * 8 + self.y * 2 + 1 - self.c, k),
        )

    def start_core(self, chunk):
        self.core_copy(jnp.int32(chunk)).start()

    def wait_core(self):
        for chunk in range(8):
            self.core_copy(jnp.int32(chunk)).wait_recv()

    def first(self):
        mine = self.x if self.x_first else self.y
        self.one = []
        for d in (2, 1, 3, 0):
            to = lax.rem(mine + d, 4)
            if self.x_first:
                total = self.parts[:, to, :, self.c] + self.core_recv[:, to]
            else:
                total = self.parts[:, :, to, self.c] + self.core_recv[:, :, to]
            if d == 0:
                self.one_sum[...] = total
            else:
                self.one_send[d] = total.astype(self.wire)
                copy = push(
                    self.one_send.at[d], self.one_recv.at[d], self.one_sems, d,
                    self.along(self.x_first, d),
                )
                copy.start()
                self.one.append(copy)

    def second(self):
        for copy in self.one:
            copy.wait_recv()
        total = self.one_sum[...]
        for d in (1, 2, 3):
            total = total + self.one_recv[d].astype(F32)
        self.one_sum[...] = total
        mine = self.y if self.x_first else self.x
        self.two = []
        for d in (2, 1, 3):
            copy = push(
                self.one_sum.at[:, lax.rem(mine + d, 4)], self.two_recv.at[d], self.two_sems, d,
                self.along(not self.x_first, d),
            )
            copy.start()
            self.two.append(copy)

    def third(self):
        g, i, k = self.here
        mine = self.y if self.x_first else self.x
        for copy in self.two:
            copy.wait_recv()
        self.two_sum[...] = (
            self.one_sum[:, mine] + self.two_recv[1] + self.two_recv[2] + self.two_recv[3]
        )
        self.three = push(
            self.two_sum.at[1 - g], self.three_recv, self.three_sems, 0, (1 - g, i, k)
        )
        self.three.start()

    def result(self):
        self.three.wait_recv()
        return self.two_sum[self.here[0]] + self.three_recv[...]

    def finish(self):
        for chunk in range(8):
            self.core_copy(jnp.int32(chunk)).wait_send()
        for copy in self.one + self.two + [self.three]:
            copy.wait_send()


N_SCATTER = 12
TRAINER_SCRATCH = [
    pltpu.VMEM((384, 1024), BF16),
    pltpu.VMEM((1024, 1024), BF16),
    pltpu.VMEM((1024, 1024), BF16),
    pltpu.VMEM((1024, 384), BF16),
    pltpu.VMEM((96, 384), BF16),
    pltpu.VMEM((4, 96, 384), BF16),
    pltpu.VMEM((4, 96, 384), BF16),
    pltpu.VMEM((4, 96, 1024), BF16),
    pltpu.VMEM((4, 96, 1024), F32),
    pltpu.VMEM((4, 96, 1024), BF16),
    pltpu.VMEM((96, 1024), F32),
    pltpu.VMEM((4, 96, 1024), BF16),
    pltpu.VMEM((4, 96, 1024), BF16),
    pltpu.VMEM((384, 1024), BF16),
    pltpu.VMEM((384, 1024), BF16),
    pltpu.VMEM((384, 1024), F32),
    pltpu.VMEM((384, 1024), BF16),
    pltpu.VMEM((4, 8, 384), F32),
    pltpu.VMEM((4, 8, 384), F32),
    pltpu.SemaphoreType.DMA((6,)),
    pltpu.SemaphoreType.DMA((2, 4)),
    pltpu.SemaphoreType.DMA((2, 4)),
    pltpu.SemaphoreType.DMA((2, 4)),
    pltpu.SemaphoreType.DMA((2, 4)),
]
N_TRAINER = len(TRAINER_SCRATCH)
for _width in (1024, 1024, 384, 384):
    TRAINER_SCRATCH += Scatter.scratch(16, _width, BF16)


def columns(n):
    return pl.ds(pl.multiple_of(n * 256, 256), 256)


def step_kernel(
    velocity, viscosity, selection, w_in_far, w_up_far, w_down_far, w_out_far,
    velocity_next, pressure, out_up, out_down, out_small, lines, fold, *refs
):
    here = place()
    g, i, k = here
    n_stencil = len(Stencil.scratch)
    step = Stencil(here, velocity_next, pressure, refs[:n_stencil])
    refs = refs[n_stencil:]
    (
        w_in, w_up, w_down, w_out, targets, in_all, err_all, lifted_b, slope, active, own_mixed,
        down_send, down_recv, back_b, back_raised, lift_sum, lift_b, tail_send, tail_recv,
        near_sems, in_sems, down_sems, err_sems, tail_sems,
    ) = refs[:N_TRAINER]
    refs = refs[N_TRAINER:]
    up, down, grad_in, grad_out = (
        Scatter(here, refs[n * N_SCATTER : (n + 1) * N_SCATTER], BF16, x_first)
        for n, x_first in enumerate((True, False, False, True))
    )
    sent = []

    def peer(d):
        return (g, i, lax.rem(k + d, 4))

    def start(copies):
        for copy in copies:
            copy.start()
        sent.extend(copies)
        return copies

    met = stencil_targets(here) + trainer_targets(here)
    greet(met)
    near = [
        pltpu.make_async_copy(src, dst, near_sems.at[n])
        for n, (src, dst) in enumerate(
            (
                (velocity, step.fields.at[0:3]),
                (viscosity, step.fields.at[3]),
                (w_in_far, w_in),
                (w_up_far, w_up),
                (w_down_far, w_down),
                (w_out_far, w_out),
            )
        )
    ]
    for copy in near:
        copy.start()
    make_fold(fold)
    for copy in near[:2]:
        copy.wait()
    pick_patches(step.fields, selection, lines, fold, in_all.at[k])
    step.prepare()
    greeted(met)
    in_copies = start(
        [push(in_all.at[k], in_all.at[k], in_sems, d, peer(d)) for d in (2, 1, 3)]
    )
    step.send_one()
    for copy in near[2:]:
        copy.wait()

    def forward(owner):
        rows = in_all[owner]
        lifted = matmul(rows, w_in[...])
        lifted_b[owner] = lifted.astype(BF16)

        def raise_(n, carry):
            at = columns(n)
            raised = matmul(lifted_b[owner], w_up[:, at])
            sigmoid = jax.nn.sigmoid(raised)
            active[owner, :, at] = (raised * sigmoid).astype(BF16)
            slope[owner, :, at] = sigmoid * (1.0 + raised * (1.0 - sigmoid))
            return carry

        lax.fori_loop(0, 4, raise_, 0)
        return lifted

    own_mixed[...] = forward(k) + matmul(active[k], w_down[...])
    step.make_source()
    step.send_two()
    down_copies = []
    for copy, d in zip(in_copies[1:] + in_copies[:1], (3, 1, 2)):
        copy.wait_recv()
        owner = lax.rem(k + d, 4)
        forward(owner)
        down_send[d] = matmul(active[owner], w_down[...]).astype(BF16)
        down_copies += start([push(down_send.at[d], down_recv.at[d], down_sems, d, peer(d))])
    step.solve()
    pick_patches(velocity_next, selection, lines, fold, targets)

    for copy in down_copies:
        copy.wait_recv()
    mixed = own_mixed[...]
    for d in (1, 2, 3):
        mixed = mixed + down_recv[d].astype(F32)
    mixed_b = mixed.astype(BF16)
    predicted = matmul(mixed_b, w_out[...])
    scale = float(24576) ** (-0.5)
    err_all[k] = ((predicted - targets[...].astype(F32)) * scale).astype(BF16)
    err_copies = start(
        [push(err_all.at[k], err_all.at[k], err_sems, d, peer(d)) for d in (2, 1, 3)]
    )
    for n in range(8):
        block = matmul_tn(mixed_b[:, 128 * n : 128 * n + 128], err_all[k])
        grad_out.parts[n // 4, n % 4] = block.reshape(4, 2, 16, 384)
        grad_out.start_core(n)
    grad_out.wait_core()
    grad_out.first()
    for copy in err_copies:
        copy.wait_recv()
    errors = err_all[...].reshape(384, 384)

    def back(n, carry):
        at = columns(n)
        both = matmul_nt(errors, w_out[at, :])
        back_b[:, at] = both.astype(BF16)
        lift_sum[:, at] = both
        return carry

    lax.fori_loop(0, 4, back, 0)

    def grad_chunk(scatter, left, right, width):
        def chunk(n, carry):
            at = pl.ds(pl.multiple_of(n * 128, 128), 128)
            block = matmul_tn(left[:, at], right)
            scatter.parts[lax.div(n, 4), lax.rem(n, 4)] = block.reshape(4, 2, 16, width)
            scatter.start_core(n)
            return carry

        lax.fori_loop(0, 8, chunk, 0)

    grad_chunk(down, back_b, active[...].reshape(384, 1024), 1024)

    def back_up(n, carry):
        at = columns(n)
        steep = slope[:, :, at].reshape(384, 256)
        back_raised[:, at] = (matmul_nt(back_b[...], w_down[at, :]) * steep).astype(BF16)
        return carry

    lax.fori_loop(0, 4, back_up, 0)
    down.wait_core()
    down.first()
    own_row = iota((384, 256), 0) // 96 == k

    def back_lift(n, carry):
        at = columns(n)
        mine = jnp.where(own_row, lift_sum[:, at], 0.0)
        lift_b[:, at] = (mine + matmul_nt(back_raised[...], w_up[at, :])).astype(BF16)
        return carry

    lax.fori_loop(0, 4, back_lift, 0)
    lifted_rows = lifted_b.reshape(384, 1024)
    grad_chunk(up, lifted_rows, back_raised[...], 1024)
    grad_chunk(grad_in, lift_b, in_all[...].reshape(384, 384), 384)
    up.wait_core()
    up.first()
    grad_in.wait_core()
    grad_in.first()
    scatters = (grad_out, down, up, grad_in)
    for scatter in scatters:
        scatter.second()
    for scatter in scatters:
        scatter.third()
    last_in, last_out = grad_in.result(), grad_out.result()
    for j in range(4):
        tail_send[j, 0:4] = last_in[4 * j : 4 * j + 4]
        tail_send[j, 4:8] = last_out[4 * j : 4 * j + 4]
    tail_copies = start(
        [
            push(tail_send.at[lax.rem(k + d, 4)], tail_recv.at[d], tail_sems, d, peer(d))
            for d in (2, 1, 3)
        ]
    )
    out_down[...] = down.result()
    out_up[...] = up.result()
    for copy in tail_copies:
        copy.wait_recv()
    out_small[...] = tail_send[k] + tail_recv[1] + tail_recv[2] + tail_recv[3]
    for copy in sent:
        copy.wait_send()
    step.finish()
    for scatter in scatters:
        scatter.finish()


def on_device(velocity, viscosity, selection, w_in, w_up, w_down, w_out):
    shape = jax.ShapeDtypeStruct
    far, near = pl.BlockSpec(memory_space=pl.ANY), pl.BlockSpec(memory_space=pltpu.VMEM)
    velocity_next, pressure, grad_up, grad_down, small = pl.pallas_call(
        step_kernel,
        out_shape=[
            shape((3, 8, 32, 128), F32),
            shape((8, 32, 128), F32),
            shape((16, 1024), F32),
            shape((16, 1024), F32),
            shape((8, 384), F32),
        ],
        in_specs=[far, far, near, far, far, far, far],
        out_specs=[near] * 5,
        scratch_shapes=PATCH_SCRATCH + Stencil.scratch + TRAINER_SCRATCH,
        compiler_params=pltpu.CompilerParams(
            collective_id=0, has_side_effects=True, vmem_limit_bytes=56 * MIB
        ),
        name="step",
    )(velocity, viscosity, selection.reshape(1, 96), w_in, w_up, w_down, w_out)
    return (velocity_next, pressure, small[:4].T, grad_up, grad_down.T, small[4:])


def solution(mesh):
    placed = (
        P(None, "gx", "gy", "grp"),
        P("gx", "gy", "grp"),
        P("grp", "gx", "gy", None),
        P(),
        P(None, "gy"),
        P("gy", None),
        P(),
    )
    return jax.shard_map(
        on_device,
        mesh=mesh,
        in_specs=placed,
        out_specs=(
            P(None, "gx", "gy", "grp"),
            P("gx", "gy", "grp"),
            P(None, ("grp", "gx", "gy")),
            P(("grp", "gx"), "gy"),
            P("gy", ("grp", "gx")),
            P(("grp", "gx", "gy"), None),
        ),
        check_vma=False,
    )
```

profile of v0, /device:TPU:32, one launch (start us, length us, event | category | flops | bytes accessed | tf_op | source)
XLA Modules:
  0.0 114.8 jit_solution(6969337488806474420)
XLA Ops:
  0.6 106.5 %step.1 = (f32[3,8,32,128]{3,2,1,0:T(8,128)}, f32[8,32,128]{2,1,0:T(8,128)}, f32[16,1024]{1,0:T(8,128)}, f32[16,1024]{1,0:T(8,128)}, f32[8,384]{1,0:T(8,128)}) custom-call(f32[3,8,32,128]{3,2,1,0:T(8,128)} %velocity.1, f32[8,32,128]{2,1,0:T(8,128)} %viscosity.1, s32[1,96]{1,0:T(1,128)} %bitcast.5, bf16[384,1024]{1,0:T(8,128)(2,1)} %w_in_far.1, ...), custom_call_target="tpu_custom_call" | custom-call | tf_op jit(solution)/shard_map/step/pallas_call | solution.py:709
  107.2 1.4 %fusion = (f32[4,384]{1,0:T(4,128)}, f32[384,4]{0,1:T(4,128)}) fusion(f32[8,384]{1,0:T(8,128)} %get-tuple-element.13), kind=kLoop, calls=%fused_computation.1 | loop fusion | bytes 24576 | tf_op jit(solution)/shard_map/slice | solution.py:726
  108.6 1.8 %copy.17 = f32[3,8,32,128]{3,2,1,0:T(8,128)} copy(f32[3,8,32,128]{3,2,1,0:T(8,128)} %get-tuple-element.24) | data formatting | bytes 786432
  110.3 1.6 %copy.18 = f32[8,32,128]{2,1,0:T(8,128)} copy(f32[8,32,128]{2,1,0:T(8,128)} %get-tuple-element.25) | data formatting | bytes 262144
  111.9 1.5 %copy.19 = f32[16,1024]{1,0:T(8,128)} copy(f32[16,1024]{1,0:T(8,128)} %get-tuple-element.27) | data formatting | bytes 131072
  113.4 1.5 %copy.20 = f32[1024,16]{0,1:T(8,128)} copy(f32[1024,16]{0,1:T(8,128)} %bitcast.4) | data formatting | bytes 131072
where the time goes:
time: 115 us
  Pallas kernels  107 us (93%)
  local copies, waits for them, and re-layouts  7.66 us (7%)
    pallas_call x1, Pallas kernels, on_device(): pl.pallas_call(step_kernel, out_shape=[shape((3, 8, 32, 128), F32), shape...  107 us
    unnamed x4, local copies, waits for them, and re-layouts  6.28 us

commit v1 on v0

--- a/solution.py
+++ b/solution.py
@@ -15,6 +15,7 @@
 PLANE = FACES + DIAGONALS
 CROSS_ONE = [(0, 0)] + FACES
 CROSS_TWO = [(0, 0)] + PLANE
+EDGE_ORDER = (1, 2, 0, 3)
 
 
 def place():
@@ -147,7 +148,7 @@
         self.y_send[0] = self.fields[:, :, 30:32, :]
         self.y_send[1] = self.fields[:, :, 0:2, :]
         for f in range(4):
-            self.z_send[f] = pack_edge(
+            self.z_send[EDGE_ORDER.index(f)] = pack_edge(
                 g, lambda part: self.fields[f, part // 2, 16 * (part % 2) : 16 * (part % 2) + 16, :]
             )
 
@@ -171,7 +172,9 @@
             copies.append(push(src, dst, self.sems_one, slot, target))
         for n, (dx, dy) in enumerate(CROSS_ONE):
             target = offset(self.here, dx, dy, True)
-            copies.append(push(self.z_send, self.z_recv.at[n], self.sems_one, len(copies), target))
+            some = slice(1, 3) if dx else (slice(0, 2) if dy else slice(0, 4))
+            src, dst = self.z_send.at[some], self.z_recv.at[n, some]
+            copies.append(push(src, dst, self.sems_one, len(copies), target))
         for copy in copies:
             copy.start()
         self.copies_one = copies
@@ -193,7 +196,7 @@
                 def store(to, row, rows, f=f):
                     wide[f, 1, to, row : row + rows.shape[0], :] = rows
 
-                unpack_block(g, self.z_recv[n, f], -dx, -dy, 2, store)
+                unpack_block(g, self.z_recv[n, EDGE_ORDER.index(f)], -dx, -dy, 2, store)
 
         @pl.when(i == 0)
         def _():
@@ -373,27 +376,28 @@
         return [
             pltpu.VMEM((2, 4, 4, 2, rows, width), F32),
             pltpu.VMEM((2, 4, 4, rows, width), F32),
-            pltpu.VMEM((4, 2, 4, rows, width), wire),
-            pltpu.VMEM((4, 2, 4, rows, width), wire),
+            pltpu.VMEM((2, 4, 4, rows, width), wire),
+            pltpu.VMEM((2, 4, 4, rows, width), wire),
             pltpu.VMEM((2, 4, rows, width), F32),
-            pltpu.VMEM((4, 2, rows, width), F32),
+            pltpu.VMEM((2, 4, rows, width), F32),
             pltpu.VMEM((2, rows, width), F32),
             pltpu.VMEM((rows, width), F32),
             pltpu.SemaphoreType.DMA((2, 8)),
-            pltpu.SemaphoreType.DMA((2, 4)),
-            pltpu.SemaphoreType.DMA((2, 4)),
+            pltpu.SemaphoreType.DMA((2, 8)),
+            pltpu.SemaphoreType.DMA((2, 8)),
             pltpu.SemaphoreType.DMA((2, 1)),
         ]
 
-    def __init__(self, here, refs, wire, x_first):
+    def __init__(self, here, refs, wire):
         g, i, k = here
-        self.here, self.wire, self.x_first = here, wire, x_first
+        self.here, self.wire = here, wire
         self.x, self.y, self.c = lax.div(i, 8), lax.rem(lax.div(i, 2), 4), lax.rem(i, 2)
         (
             self.parts, self.core_recv, self.one_send, self.one_recv, self.one_sum,
             self.two_recv, self.two_sum, self.three_recv,
             self.core_sems, self.one_sems, self.two_sems, self.three_sems,
         ) = refs
+        self.one, self.two = ([], []), ([], [])
 
     def along(self, on_x, d):
         g, i, k = self.here
@@ -418,55 +422,53 @@
     def start_core(self, chunk):
         self.core_copy(jnp.int32(chunk)).start()
 
-    def wait_core(self):
-        for chunk in range(8):
+    def first(self, half):
+        for chunk in range(4 * half, 4 * half + 4):
             self.core_copy(jnp.int32(chunk)).wait_recv()
-
-    def first(self):
-        mine = self.x if self.x_first else self.y
-        self.one = []
+        mine = self.y if half else self.x
         for d in (2, 1, 3, 0):
             to = lax.rem(mine + d, 4)
-            if self.x_first:
-                total = self.parts[:, to, :, self.c] + self.core_recv[:, to]
+            if half:
+                total = self.parts[half, :, to, self.c] + self.core_recv[half, :, to]
             else:
-                total = self.parts[:, :, to, self.c] + self.core_recv[:, :, to]
+                total = self.parts[half, to, :, self.c] + self.core_recv[half, to]
             if d == 0:
-                self.one_sum[...] = total
+                self.one_sum[half] = total
             else:
-                self.one_send[d] = total.astype(self.wire)
+                self.one_send[half, d] = total.astype(self.wire)
                 copy = push(
-                    self.one_send.at[d], self.one_recv.at[d], self.one_sems, d,
-                    self.along(self.x_first, d),
+                    self.one_send.at[half, d], self.one_recv.at[half, d], self.one_sems,
+                    4 * half + d, self.along(not half, d),
                 )
                 copy.start()
-                self.one.append(copy)
-
-    def second(self):
-        for copy in self.one:
+                self.one[half].append(copy)
+
+    def second(self, half):
+        for copy in self.one[half]:
             copy.wait_recv()
-        total = self.one_sum[...]
+        total = self.one_sum[half]
         for d in (1, 2, 3):
-            total = total + self.one_recv[d].astype(F32)
-        self.one_sum[...] = total
-        mine = self.y if self.x_first else self.x
-        self.two = []
+            total = total + self.one_recv[half, d].astype(F32)
+        self.one_sum[half] = total
+        mine = self.x if half else self.y
         for d in (2, 1, 3):
             copy = push(
-                self.one_sum.at[:, lax.rem(mine + d, 4)], self.two_recv.at[d], self.two_sems, d,
-                self.along(not self.x_first, d),
+                self.one_sum.at[half, lax.rem(mine + d, 4)], self.two_recv.at[half, d],
+                self.two_sems, 4 * half + d, self.along(half, d),
             )
             copy.start()
-            self.two.append(copy)
+            self.two[half].append(copy)
 
     def third(self):
         g, i, k = self.here
-        mine = self.y if self.x_first else self.x
-        for copy in self.two:
-            copy.wait_recv()
-        self.two_sum[...] = (
-            self.one_sum[:, mine] + self.two_recv[1] + self.two_recv[2] + self.two_recv[3]
-        )
+        for half in (0, 1):
+            mine = self.x if half else self.y
+            for copy in self.two[half]:
+                copy.wait_recv()
+            total = self.one_sum[half, mine]
+            for d in (1, 2, 3):
+                total = total + self.two_recv[half, d]
+            self.two_sum[half] = total
         self.three = push(
             self.two_sum.at[1 - g], self.three_recv, self.three_sems, 0, (1 - g, i, k)
         )
@@ -479,7 +481,7 @@
     def finish(self):
         for chunk in range(8):
             self.core_copy(jnp.int32(chunk)).wait_send()
-        for copy in self.one + self.two + [self.three]:
+        for copy in self.one[0] + self.one[1] + self.two[0] + self.two[1] + [self.three]:
             copy.wait_send()
 
 
@@ -495,9 +497,10 @@
     pltpu.VMEM((4, 96, 1024), BF16),
     pltpu.VMEM((4, 96, 1024), F32),
     pltpu.VMEM((4, 96, 1024), BF16),
-    pltpu.VMEM((96, 1024), F32),
     pltpu.VMEM((4, 96, 1024), BF16),
-    pltpu.VMEM((4, 96, 1024), BF16),
+    pltpu.VMEM((96, 384), F32),
+    pltpu.VMEM((4, 96, 384), BF16),
+    pltpu.VMEM((4, 96, 384), BF16),
     pltpu.VMEM((384, 1024), BF16),
     pltpu.VMEM((384, 1024), BF16),
     pltpu.VMEM((384, 1024), F32),
@@ -529,14 +532,13 @@
     step = Stencil(here, velocity_next, pressure, refs[:n_stencil])
     refs = refs[n_stencil:]
     (
-        w_in, w_up, w_down, w_out, targets, in_all, err_all, lifted_b, slope, active, own_mixed,
-        down_send, down_recv, back_b, back_raised, lift_sum, lift_b, tail_send, tail_recv,
+        w_in, w_up, w_down, w_out, targets, in_all, err_all, lifted_b, slope, active, mixed,
+        own_predicted, down_send, down_recv, back_b, back_raised, lift_sum, lift_b, tail_send, tail_recv,
         near_sems, in_sems, down_sems, err_sems, tail_sems,
     ) = refs[:N_TRAINER]
     refs = refs[N_TRAINER:]
     up, down, grad_in, grad_out = (
-        Scatter(here, refs[n * N_SCATTER : (n + 1) * N_SCATTER], BF16, x_first)
-        for n, x_first in enumerate((True, False, False, True))
+        Scatter(here, refs[n * N_SCATTER : (n + 1) * N_SCATTER], BF16) for n in range(4)
     )
     sent = []
 
@@ -579,7 +581,7 @@
     for copy in near[2:]:
         copy.wait()
 
-    def forward(owner):
+    def forward(owner, own):
         rows = in_all[owner]
         lifted = matmul(rows, w_in[...])
         lifted_b[owner] = lifted.astype(BF16)
@@ -593,42 +595,44 @@
             return carry
 
         lax.fori_loop(0, 4, raise_, 0)
-        return lifted
-
-    own_mixed[...] = forward(k) + matmul(active[k], w_down[...])
+        part = matmul(active[owner], w_down[...])
+        mixed[owner] = (lifted + part if own else part).astype(BF16)
+        return matmul(mixed[owner], w_out[...])
+
+    own_predicted[...] = forward(k, True)
     step.make_source()
     step.send_two()
     down_copies = []
     for copy, d in zip(in_copies[1:] + in_copies[:1], (3, 1, 2)):
         copy.wait_recv()
-        owner = lax.rem(k + d, 4)
-        forward(owner)
-        down_send[d] = matmul(active[owner], w_down[...]).astype(BF16)
+        down_send[d] = forward(lax.rem(k + d, 4), False).astype(BF16)
         down_copies += start([push(down_send.at[d], down_recv.at[d], down_sems, d, peer(d))])
     step.solve()
     pick_patches(velocity_next, selection, lines, fold, targets)
 
     for copy in down_copies:
         copy.wait_recv()
-    mixed = own_mixed[...]
+    predicted = own_predicted[...]
     for d in (1, 2, 3):
-        mixed = mixed + down_recv[d].astype(F32)
-    mixed_b = mixed.astype(BF16)
-    predicted = matmul(mixed_b, w_out[...])
+        predicted = predicted + down_recv[d].astype(F32)
     scale = float(24576) ** (-0.5)
     err_all[k] = ((predicted - targets[...].astype(F32)) * scale).astype(BF16)
     err_copies = start(
         [push(err_all.at[k], err_all.at[k], err_sems, d, peer(d)) for d in (2, 1, 3)]
     )
-    for n in range(8):
-        block = matmul_tn(mixed_b[:, 128 * n : 128 * n + 128], err_all[k])
-        grad_out.parts[n // 4, n % 4] = block.reshape(4, 2, 16, 384)
-        grad_out.start_core(n)
-    grad_out.wait_core()
-    grad_out.first()
     for copy in err_copies:
         copy.wait_recv()
     errors = err_all[...].reshape(384, 384)
+
+    def grad_chunk(scatter, half, left, right, width):
+        def chunk(n, carry):
+            at = pl.ds(pl.multiple_of(n * 128, 128), 128)
+            block = matmul_tn(left[:, at], right)
+            scatter.parts[half, n - 4 * half] = block.reshape(4, 2, 16, width)
+            scatter.start_core(n)
+            return carry
+
+        lax.fori_loop(4 * half, 4 * half + 4, chunk, 0)
 
     def back(n, carry):
         at = columns(n)
@@ -639,18 +643,6 @@
 
     lax.fori_loop(0, 4, back, 0)
 
-    def grad_chunk(scatter, left, right, width):
-        def chunk(n, carry):
-            at = pl.ds(pl.multiple_of(n * 128, 128), 128)
-            block = matmul_tn(left[:, at], right)
-            scatter.parts[lax.div(n, 4), lax.rem(n, 4)] = block.reshape(4, 2, 16, width)
-            scatter.start_core(n)
-            return carry
-
-        lax.fori_loop(0, 8, chunk, 0)
-
-    grad_chunk(down, back_b, active[...].reshape(384, 1024), 1024)
-
     def back_up(n, carry):
         at = columns(n)
         steep = slope[:, :, at].reshape(384, 256)
@@ -658,27 +650,40 @@
         return carry
 
     lax.fori_loop(0, 4, back_up, 0)
-    down.wait_core()
-    down.first()
+    lifted_rows = lifted_b.reshape(384, 1024)
+    mixed_rows = mixed.reshape(384, 1024)
+    raised_rows = back_raised[...]
+    grad_chunk(up, 0, lifted_rows, raised_rows, 1024)
+    grad_chunk(up, 1, lifted_rows, raised_rows, 1024)
+    up.first(0)
+    grad_chunk(grad_out, 0, mixed_rows, errors, 384)
+    grad_chunk(grad_out, 1, mixed_rows, errors, 384)
+    up.first(1)
     own_row = iota((384, 256), 0) // 96 == k
 
     def back_lift(n, carry):
         at = columns(n)
         mine = jnp.where(own_row, lift_sum[:, at], 0.0)
-        lift_b[:, at] = (mine + matmul_nt(back_raised[...], w_up[at, :])).astype(BF16)
+        lift_b[:, at] = (mine + matmul_nt(raised_rows, w_up[at, :])).astype(BF16)
         return carry
 
     lax.fori_loop(0, 4, back_lift, 0)
-    lifted_rows = lifted_b.reshape(384, 1024)
-    grad_chunk(up, lifted_rows, back_raised[...], 1024)
-    grad_chunk(grad_in, lift_b, in_all[...].reshape(384, 384), 384)
-    up.wait_core()
-    up.first()
-    grad_in.wait_core()
-    grad_in.first()
-    scatters = (grad_out, down, up, grad_in)
+    grad_out.first(0)
+    grad_out.first(1)
+    rows_in = in_all[...].reshape(384, 384)
+    grad_chunk(grad_in, 0, lift_b, rows_in, 384)
+    grad_chunk(grad_in, 1, lift_b, rows_in, 384)
+    active_rows = active[...].reshape(384, 1024)
+    grad_chunk(down, 0, back_b, active_rows, 1024)
+    grad_in.first(0)
+    grad_in.first(1)
+    grad_chunk(down, 1, back_b, active_rows, 1024)
+    down.first(0)
+    down.first(1)
+    scatters = (up, grad_out, grad_in, down)
     for scatter in scatters:
-        scatter.second()
+        scatter.second(0)
+        scatter.second(1)
     for scatter in scatters:
         scatter.third()
     last_in, last_out = grad_in.result(), grad_out.result()
@@ -703,6 +708,18 @@
         scatter.finish()
 
 
+def emit_kernel(
+    near_next, near_pressure, near_up, near_down, near_small,
+    velocity_next, pressure, grad_up, grad_down, first, second,
+):
+    velocity_next[...] = near_next[...]
+    pressure[...] = near_pressure[...]
+    grad_up[...] = near_up[...]
+    grad_down[...] = near_down[...]
+    first[...] = near_small[0:4]
+    second[...] = near_small[4:8]
+
+
 def on_device(velocity, viscosity, selection, w_in, w_up, w_down, w_out):
     shape = jax.ShapeDtypeStruct
     far, near = pl.BlockSpec(memory_space=pl.ANY), pl.BlockSpec(memory_space=pltpu.VMEM)
@@ -723,7 +740,22 @@
         ),
         name="step",
     )(velocity, viscosity, selection.reshape(1, 96), w_in, w_up, w_down, w_out)
-    return (velocity_next, pressure, small[:4].T, grad_up, grad_down.T, small[4:])
+    velocity_next, pressure, grad_up, grad_down, first, second = pl.pallas_call(
+        emit_kernel,
+        out_shape=[
+            shape((3, 8, 32, 128), F32),
+            shape((8, 32, 128), F32),
+            shape((16, 1024), F32),
+            shape((16, 1024), F32),
+            shape((4, 384), F32),
+            shape((4, 384), F32),
+        ],
+        in_specs=[near] * 5,
+        out_specs=[near] * 6,
+        compiler_params=pltpu.CompilerParams(vmem_limit_bytes=60 * MIB),
+        name="emit",
+    )(velocity_next, pressure, grad_up, grad_down, small)
+    return (velocity_next, pressure, first.T, grad_up, grad_down.T, second)
 
 
 def solution(mesh):

time: 115 us -> 98.8 us (0.86); the launches traced: 115 us -> 97.2 us
  Pallas kernels: 107 us -> 96.5 us
  local copies, waits for them, and re-layouts: 7.66 us -> 0 us
    pallas_call x1, Pallas kernels: 107 us -> 94.6 us  [on_device(): pl.pallas_call(step_kernel, out_shape=[shape((3, 8, 32, 128), F32), shape...]
    unnamed x4 -> x0, local copies, waits for them, and re-layouts: 6.28 us -> none
    pallas_call x0 -> x1, Pallas kernels: none -> 1.95 us  [on_device(): pl.pallas_call(emit_kernel, out_shape=[shape((3, 8, 32, 128), F32), shape...]
    slice x1 -> x0, local copies, waits for them, and re-layouts: 1.38 us -> none  [on_device(): small[4:]]
where the time goes in v1:
time: 98.8 us; the launch traced here: 97.2 us
  Pallas kernels  96.5 us (98%)
    pallas_call x1, Pallas kernels, on_device(): pl.pallas_call(step_kernel, out_shape=[shape((3, 8, 32, 128), F32), shape...  94.6 us

profile of v1, /device:TPU:32, one launch (start us, length us, event | category | flops | bytes accessed | tf_op | source)
XLA Modules:
  0.0 97.2 jit_solution(3245156610947518629)
XLA Ops:
  0.6 94.6 %step.1 = (f32[3,8,32,128]{3,2,1,0:T(8,128)}, f32[8,32,128]{2,1,0:T(8,128)}, f32[16,1024]{1,0:T(8,128)}, f32[16,1024]{1,0:T(8,128)}, f32[8,384]{1,0:T(8,128)}) custom-call(f32[3,8,32,128]{3,2,1,0:T(8,128)} %velocity.1, f32[8,32,128]{2,1,0:T(8,128)} %viscosity.1, s32[1,96]{1,0:T(1,128)} %bitcast.3, bf16[384,1024]{1,0:T(8,128)(2,1)} %w_in_far.1, ...), custom_call_target="tpu_custom_call" | custom-call | tf_op jit(solution)/shard_map/step/pallas_call | solution.py:726
  95.2 1.9 %emit.1 = (f32[3,8,32,128]{3,2,1,0:T(8,128)}, f32[8,32,128]{2,1,0:T(8,128)}, f32[16,1024]{1,0:T(8,128)}, f32[16,1024]{1,0:T(8,128)}, f32[4,384]{1,0:T(4,128)}, /*index=5*/f32[4,384]{1,0:T(4,128)}) custom-call(f32[3,8,32,128]{3,2,1,0:T(8,128)} %get-tuple-element.17.near_next, f32[8,32,128]{2,1,0:T(8,128)} %get-tuple-element.18.near_pressure, ...), custom_call_target="tpu_custom_call" | custom-call | tf_op jit(solution)/shard_map/emit/pallas_call | solution.py:743

commit v2 on v1

--- a/solution.py
+++ b/solution.py
@@ -367,6 +367,8 @@
     out = [(g, i, lax.rem(k + d, 4)) for d in (1, 2, 3)]
     out += [(g, lax.rem(x + d, 4) * 8 + y * 2 + c, k) for d in (1, 2, 3)]
     out += [(g, x * 8 + lax.rem(y + d, 4) * 2 + c, k) for d in (1, 2, 3)]
+    out += [(g, lax.rem(x + d, 4) * 8 + y * 2 + 1 - c, k) for d in (1, 2, 3)]
+    out += [(g, x * 8 + lax.rem(y + d, 4) * 2 + 1 - c, k) for d in (1, 2, 3)]
     return out + [(g, x * 8 + y * 2 + 1 - c, k), (1 - g, i, k)]
 
 
@@ -379,7 +381,8 @@
             pltpu.VMEM((2, 4, 4, rows, width), wire),
             pltpu.VMEM((2, 4, 4, rows, width), wire),
             pltpu.VMEM((2, 4, rows, width), F32),
-            pltpu.VMEM((2, 4, rows, width), F32),
+            pltpu.VMEM((2, 4, rows, width), wire),
+            pltpu.VMEM((2, 4, rows, width), wire),
             pltpu.VMEM((2, rows, width), F32),
             pltpu.VMEM((rows, width), F32),
             pltpu.SemaphoreType.DMA((2, 8)),
@@ -394,7 +397,7 @@
         self.x, self.y, self.c = lax.div(i, 8), lax.rem(lax.div(i, 2), 4), lax.rem(i, 2)
         (
             self.parts, self.core_recv, self.one_send, self.one_recv, self.one_sum,
-            self.two_recv, self.two_sum, self.three_recv,
+            self.two_send, self.two_recv, self.two_sum, self.three_recv,
             self.core_sems, self.one_sems, self.two_sems, self.three_sems,
         ) = refs
         self.one, self.two = ([], []), ([], [])
@@ -420,7 +423,7 @@
         )
 
     def start_core(self, chunk):
-        self.core_copy(jnp.int32(chunk)).start()
+        self.core_copy(chunk).start()
 
     def first(self, half):
         for chunk in range(4 * half, 4 * half + 4):
@@ -450,10 +453,11 @@
         for d in (1, 2, 3):
             total = total + self.one_recv[half, d].astype(F32)
         self.one_sum[half] = total
+        self.two_send[half] = total.astype(self.wire)
         mine = self.x if half else self.y
         for d in (2, 1, 3):
             copy = push(
-                self.one_sum.at[half, lax.rem(mine + d, 4)], self.two_recv.at[half, d],
+                self.two_send.at[half, lax.rem(mine + d, 4)], self.two_recv.at[half, d],
                 self.two_sems, 4 * half + d, self.along(half, d),
             )
             copy.start()
@@ -467,7 +471,7 @@
                 copy.wait_recv()
             total = self.one_sum[half, mine]
             for d in (1, 2, 3):
-                total = total + self.two_recv[half, d]
+                total = total + self.two_recv[half, d].astype(F32)
             self.two_sum[half] = total
         self.three = push(
             self.two_sum.at[1 - g], self.three_recv, self.three_sems, 0, (1 - g, i, k)
@@ -485,7 +489,145 @@
             copy.wait_send()
 
 
-N_SCATTER = 12
+class Product:
+    scratch = [
+        pltpu.VMEM((4, 2, 128, 384), F32),
+        pltpu.VMEM((4, 128, 384), F32),
+        pltpu.VMEM((4, 128, 384), BF16),
+        pltpu.VMEM((4, 128, 384), BF16),
+        pltpu.VMEM((128, 384), F32),
+        pltpu.VMEM((2, 4, 4, 2, 16, 128), F32),
+        pltpu.VMEM((4, 2, 4, 2, 16, 128), BF16),
+        pltpu.VMEM((4, 2, 4, 2, 16, 128), BF16),
+        pltpu.VMEM((2, 4, 2, 16, 128), F32),
+        pltpu.VMEM((4, 2, 16, 128), F32),
+        pltpu.VMEM((4, 2, 16, 128), F32),
+        pltpu.VMEM((4, 2, 16, 128), F32),
+        pltpu.SemaphoreType.DMA((2, 4)),
+        pltpu.SemaphoreType.DMA((2, 4)),
+        pltpu.SemaphoreType.DMA((2, 4)),
+        pltpu.SemaphoreType.DMA((2, 1)),
+        pltpu.SemaphoreType.DMA((2, 8)),
+    ]
+
+    def __init__(self, here, refs, on_x):
+        g, i, k = here
+        self.here, self.on_x = here, on_x
+        self.x, self.y, self.c = lax.div(i, 8), lax.rem(lax.div(i, 2), 4), lax.rem(i, 2)
+        self.mine, self.other = (self.x, self.y) if on_x else (self.y, self.x)
+        (
+            self.parts, self.core_recv, self.one_send, self.one_recv, self.one_sum, self.wide,
+            self.two_send, self.two_recv, self.two_sum, self.three_recv, self.three_sum,
+            self.four_recv, self.core_sems, self.one_sems, self.two_sems, self.three_sems,
+            self.four_sems,
+        ) = refs
+        self.copies = []
+
+    def target(self, first, second, core):
+        g, i, k = self.here
+        first, second = lax.rem(self.mine + first, 4), lax.rem(self.other + second, 4)
+        x, y = (first, second) if self.on_x else (second, first)
+        return (g, x * 8 + y * 2 + lax.rem(self.c + core, 2), k)
+
+    def core_copy(self, chunk):
+        return push(
+            self.parts.at[chunk, 1 - self.c], self.core_recv.at[chunk], self.core_sems, chunk,
+            self.target(0, 0, 1),
+        )
+
+    def start(self, copy):
+        copy.start()
+        self.copies.append(copy)
+        return copy
+
+    def fill(self, left, right):
+        def chunk(n, carry):
+            at = pl.ds(pl.multiple_of(n * 256, 256), 256)
+            self.parts[n] = matmul_tn(left[:, at], right).reshape(2, 128, 384)
+            self.core_copy(n).start()
+            return carry
+
+        lax.fori_loop(0, 4, chunk, 0)
+
+    def first(self):
+        for chunk in range(4):
+            self.core_copy(jnp.int32(chunk)).wait_recv()
+        self.one = []
+        for d in (2, 1, 3, 0):
+            to = lax.rem(self.mine + d, 4)
+            total = self.parts[to, self.c] + self.core_recv[to]
+            if d == 0:
+                self.one_sum[...] = total
+            else:
+                self.one_send[d] = total.astype(BF16)
+                copy = push(
+                    self.one_send.at[d], self.one_recv.at[d], self.one_sems, d,
+                    self.target(d, 0, 0),
+                )
+                self.one.append(self.start(copy))
+
+    def own_rows(self, at):
+        return self.wide[:, :, at] if self.on_x else self.wide[:, at]
+
+    def second(self, weights):
+        for copy in self.one:
+            copy.wait_recv()
+        total = self.one_sum[...]
+        for d in (1, 2, 3):
+            total = total + self.one_recv[d].astype(F32)
+        high = total.astype(BF16)
+        low = (total - high.astype(F32)).astype(BF16)
+        product = matmul_nt(weights, high) + matmul_nt(weights, low)
+        self.wide[...] = product.reshape(2, 4, 4, 2, 16, 128)
+        self.two = []
+        for d in (2, 1, 3):
+            self.two_send[d] = self.own_rows(lax.rem(self.other + d, 4)).astype(BF16)
+            copy = push(
+                self.two_send.at[d], self.two_recv.at[d], self.two_sems, d, self.target(0, d, 0)
+            )
+            self.two.append(self.start(copy))
+
+    def third(self):
+        g, i, k = self.here
+        for copy in self.two:
+            copy.wait_recv()
+        total = self.own_rows(self.other)
+        for d in (1, 2, 3):
+            total = total + self.two_recv[d].astype(F32)
+        self.two_sum[...] = total
+        self.three = self.start(
+            push(self.two_sum.at[1 - g], self.three_recv, self.three_sems, 0, (1 - g, i, k))
+        )
+
+    def fourth(self):
+        self.three.wait_recv()
+        self.three_sum[...] = self.two_sum[self.here[0]] + self.three_recv[...]
+        self.four = []
+        for d, core in ((2, 0), (2, 1), (1, 0), (1, 1), (3, 0), (3, 1), (0, 1)):
+            src = self.three_sum.at[lax.rem(self.mine + d, 4), lax.rem(self.c + core, 2)]
+            copy = push(
+                src, self.four_recv.at[self.mine, self.c], self.four_sems, 2 * d + core,
+                self.target(d, 0, core),
+            )
+            self.four.append(self.start(copy))
+        self.four_recv[self.mine, self.c] = self.three_sum[self.mine, self.c]
+
+    def result(self, out):
+        for copy in self.four:
+            copy.wait_recv()
+        for first in range(4):
+            for core in range(2):
+                at = 128 * (2 * first + core)
+                out[:, at : at + 128] = self.four_recv[first, core]
+
+    def finish(self):
+        for chunk in range(4):
+            self.core_copy(jnp.int32(chunk)).wait_send()
+        for copy in self.copies:
+            copy.wait_send()
+
+
+N_SCATTER = 13
 TRAINER_SCRATCH = [
     pltpu.VMEM((384, 1024), BF16),
     pltpu.VMEM((1024, 1024), BF16),
@@ -494,17 +636,18 @@
     pltpu.VMEM((96, 384), BF16),
     pltpu.VMEM((4, 96, 384), BF16),
     pltpu.VMEM((4, 96, 384), BF16),
-    pltpu.VMEM((4, 96, 1024), BF16),
+    pltpu.VMEM((96, 1024), BF16),
     pltpu.VMEM((4, 96, 1024), F32),
     pltpu.VMEM((4, 96, 1024), BF16),
     pltpu.VMEM((4, 96, 1024), BF16),
     pltpu.VMEM((96, 384), F32),
     pltpu.VMEM((4, 96, 384), BF16),
     pltpu.VMEM((4, 96, 384), BF16),
-    pltpu.VMEM((384, 1024), BF16),
-    pltpu.VMEM((384, 1024), BF16),
-    pltpu.VMEM((384, 1024), F32),
-    pltpu.VMEM((384, 1024), BF16),
+    pltpu.VMEM((4, 96, 1024), BF16),
+    pltpu.VMEM((4, 96, 1024), BF16),
+    pltpu.VMEM((96, 1024), BF16),
+    pltpu.VMEM((96, 1024), F32),
+    pltpu.VMEM((1024, 384), BF16),
     pltpu.VMEM((4, 8, 384), F32),
     pltpu.VMEM((4, 8, 384), F32),
     pltpu.SemaphoreType.DMA((6,)),
@@ -514,8 +657,7 @@
     pltpu.SemaphoreType.DMA((2, 4)),
 ]
 N_TRAINER = len(TRAINER_SCRATCH)
-for _width in (1024, 1024, 384, 384):
-    TRAINER_SCRATCH += Scatter.scratch(16, _width, BF16)
+TRAINER_SCRATCH += Scatter.scratch(16, 384, BF16) * 2 + Product.scratch * 2
 
 
 def columns(n):
@@ -533,12 +675,17 @@
     refs = refs[n_stencil:]
     (
         w_in, w_up, w_down, w_out, targets, in_all, err_all, lifted_b, slope, active, mixed,
-        own_predicted, down_send, down_recv, back_b, back_raised, lift_sum, lift_b, tail_send, tail_recv,
+        own_predicted, down_send, down_recv, back_raised, lift_b, back_b, own_back, w_in_t, tail_send, tail_recv,
         near_sems, in_sems, down_sems, err_sems, tail_sems,
     ) = refs[:N_TRAINER]
     refs = refs[N_TRAINER:]
-    up, down, grad_in, grad_out = (
-        Scatter(here, refs[n * N_SCATTER : (n + 1) * N_SCATTER], BF16) for n in range(4)
+    grad_in, grad_out = (
+        Scatter(here, refs[n * N_SCATTER : (n + 1) * N_SCATTER], BF16) for n in range(2)
+    )
+    refs = refs[2 * N_SCATTER :]
+    up, down = (
+        Product(here, refs[: len(Product.scratch)], True),
+        Product(here, refs[len(Product.scratch) :], False),
     )
     sent = []
 
@@ -574,21 +721,21 @@
     pick_patches(step.fields, selection, lines, fold, in_all.at[k])
     step.prepare()
     greeted(met)
+    step.send_one()
     in_copies = start(
         [push(in_all.at[k], in_all.at[k], in_sems, d, peer(d)) for d in (2, 1, 3)]
     )
-    step.send_one()
     for copy in near[2:]:
         copy.wait()
 
     def forward(owner, own):
         rows = in_all[owner]
         lifted = matmul(rows, w_in[...])
-        lifted_b[owner] = lifted.astype(BF16)
+        lifted_b[...] = lifted.astype(BF16)
 
         def raise_(n, carry):
             at = columns(n)
-            raised = matmul(lifted_b[owner], w_up[:, at])
+            raised = matmul(lifted_b[...], w_up[:, at])
             sigmoid = jax.nn.sigmoid(raised)
             active[owner, :, at] = (raised * sigmoid).astype(BF16)
             slope[owner, :, at] = sigmoid * (1.0 + raised * (1.0 - sigmoid))
@@ -600,6 +747,7 @@
         return matmul(mixed[owner], w_out[...])
 
     own_predicted[...] = forward(k, True)
+    w_in_t[...] = w_in[...].T
     step.make_source()
     step.send_two()
     down_copies = []
@@ -620,72 +768,77 @@
     err_copies = start(
         [push(err_all.at[k], err_all.at[k], err_sems, d, peer(d)) for d in (2, 1, 3)]
     )
-    for copy in err_copies:
+    def backward(owner, own):
+        errors = err_all[owner]
+
+        def back(n, carry):
+            at = columns(n)
+            both = matmul_nt(errors, w_out[at, :])
+            back_b[:, at] = both.astype(BF16)
+            if own:
+                own_back[:, at] = both
+            return carry
+
+        lax.fori_loop(0, 4, back, 0)
+
+        def back_up(n, carry):
+            at = columns(n)
+            steep = matmul_nt(back_b[...], w_down[at, :])
+            back_raised[owner, :, at] = (steep * slope[owner, :, at]).astype(BF16)
+            return carry
+
+        lax.fori_loop(0, 4, back_up, 0)
+
+    def lift(owner, own):
+        part = matmul_nt(back_raised[owner], w_up[...])
+        lift_b[owner] = (part + own_back[...] if own else part).astype(BF16)
+
+    backward(k, True)
+    lift(k, True)
+    for copy, d in zip(err_copies[1:], (3, 1)):
         copy.wait_recv()
+        owner = lax.rem(k + d, 4)
+        backward(owner, False)
+        lift(owner, False)
+    err_copies[0].wait_recv()
+    owner = lax.rem(k + 2, 4)
+    backward(owner, False)
+    rows_in = in_all[...].reshape(384, 384)
     errors = err_all[...].reshape(384, 384)
-
-    def grad_chunk(scatter, half, left, right, width):
+    up.fill(back_raised.reshape(384, 1024), rows_in)
+    down.fill(active.reshape(384, 1024), errors)
+
+    def grad_chunk(scatter, left, right):
         def chunk(n, carry):
-            at = pl.ds(pl.multiple_of(n * 128, 128), 128)
-            block = matmul_tn(left[:, at], right)
-            scatter.parts[half, n - 4 * half] = block.reshape(4, 2, 16, width)
-            scatter.start_core(n)
+            at = pl.ds(pl.multiple_of(n * 256, 256), 256)
+            block = matmul_tn(left[:, at], right).reshape(2, 4, 2, 16, 384)
+            for part in range(2):
+                scatter.parts[lax.div(n, 2), lax.rem(n, 2) * 2 + part] = block[part]
+                scatter.start_core(n * 2 + part)
             return carry
 
-        lax.fori_loop(4 * half, 4 * half + 4, chunk, 0)
-
-    def back(n, carry):
-        at = columns(n)
-        both = matmul_nt(errors, w_out[at, :])
-        back_b[:, at] = both.astype(BF16)
-        lift_sum[:, at] = both
-        return carry
-
-    lax.fori_loop(0, 4, back, 0)
-
-    def back_up(n, carry):
-        at = columns(n)
-        steep = slope[:, :, at].reshape(384, 256)
-        back_raised[:, at] = (matmul_nt(back_b[...], w_down[at, :]) * steep).astype(BF16)
-        return carry
-
-    lax.fori_loop(0, 4, back_up, 0)
-    lifted_rows = lifted_b.reshape(384, 1024)
-    mixed_rows = mixed.reshape(384, 1024)
-    raised_rows = back_raised[...]
-    grad_chunk(up, 0, lifted_rows, raised_rows, 1024)
-    grad_chunk(up, 1, lifted_rows, raised_rows, 1024)
-    up.first(0)
-    grad_chunk(grad_out, 0, mixed_rows, errors, 384)
-    grad_chunk(grad_out, 1, mixed_rows, errors, 384)
-    up.first(1)
-    own_row = iota((384, 256), 0) // 96 == k
-
-    def back_lift(n, carry):
-        at = columns(n)
-        mine = jnp.where(own_row, lift_sum[:, at], 0.0)
-        lift_b[:, at] = (mine + matmul_nt(raised_rows, w_up[at, :])).astype(BF16)
-        return carry
-
-    lax.fori_loop(0, 4, back_lift, 0)
-    grad_out.first(0)
-    grad_out.first(1)
-    rows_in = in_all[...].reshape(384, 384)
-    grad_chunk(grad_in, 0, lift_b, rows_in, 384)
-    grad_chunk(grad_in, 1, lift_b, rows_in, 384)
-    active_rows = active[...].reshape(384, 1024)
-    grad_chunk(down, 0, back_b, active_rows, 1024)
-    grad_in.first(0)
-    grad_in.first(1)
-    grad_chunk(down, 1, back_b, active_rows, 1024)
-    down.first(0)
-    down.first(1)
-    scatters = (up, grad_out, grad_in, down)
+        lax.fori_loop(0, 4, chunk, 0)
+
+    lift(owner, False)
+    up.first()
+    grad_chunk(grad_in, lift_b.reshape(384, 1024), rows_in)
+    down.first()
+    grad_chunk(grad_out, mixed.reshape(384, 1024), errors)
+    scatters = (grad_in, grad_out)
+    for scatter in scatters:
+        scatter.first(0)
+        scatter.first(1)
+    up.second(w_in_t[...])
+    down.second(w_out[...])
     for scatter in scatters:
         scatter.second(0)
         scatter.second(1)
+    up.third()
+    down.third()
     for scatter in scatters:
         scatter.third()
+    up.fourth()
+    down.fourth()
     last_in, last_out = grad_in.result(), grad_out.result()
     for j in range(4):
         tail_send[j, 0:4] = last_in[4 * j : 4 * j + 4]
@@ -696,15 +849,15 @@
             for d in (2, 1, 3)
         ]
     )
-    out_down[...] = down.result()
-    out_up[...] = up.result()
+    up.result(out_up)
+    down.result(out_down)
     for copy in tail_copies:
         copy.wait_recv()
     out_small[...] = tail_send[k] + tail_recv[1] + tail_recv[2] + tail_recv[3]
     for copy in sent:
         copy.wait_send()
     step.finish()
-    for scatter in scatters:
+    for scatter in scatters + (up, down):
         scatter.finish()
 
 

time: 98.8 us -> 91.3 us (0.924); the launches traced: 97.2 us -> 90.7 us
  Pallas kernels: 96.5 us -> 90 us
    pallas_call x1, Pallas kernels: 94.6 us -> 88.1 us  [on_device(): pl.pallas_call(step_kernel, out_shape=[shape((3, 8, 32, 128), F32), shape...]
where the time goes in v2:
time: 91.3 us; the launch traced here: 90.7 us
  Pallas kernels  90 us (99%)
    pallas_call x1, Pallas kernels, on_device(): pl.pallas_call(step_kernel, out_shape=[shape((3, 8, 32, 128), F32), shape...  88.1 us
    pallas_call x1, Pallas kernels, on_device(): pl.pallas_call(emit_kernel, out_shape=[shape((3, 8, 32, 128), F32), shape...  1.95 us

profile of v2, /device:TPU:32, one launch (start us, length us, event | category | flops | bytes accessed | tf_op | source)
XLA Modules:
  0.0 90.7 jit_solution(8801588150367088233)
XLA Ops:
  0.6 88.1 %step.1 = (f32[3,8,32,128]{3,2,1,0:T(8,128)}, f32[8,32,128]{2,1,0:T(8,128)}, f32[16,1024]{1,0:T(8,128)}, f32[16,1024]{1,0:T(8,128)}, f32[8,384]{1,0:T(8,128)}) custom-call(f32[3,8,32,128]{3,2,1,0:T(8,128)} %velocity.1, f32[8,32,128]{2,1,0:T(8,128)} %viscosity.1, s32[1,96]{1,0:T(1,128)} %bitcast.3, bf16[384,1024]{1,0:T(8,128)(2,1)} %w_in_far.1, ...), custom_call_target="tpu_custom_call" | custom-call | tf_op jit(solution)/shard_map/step/pallas_call | solution.py:879
  88.7 1.9 %emit.1 = (f32[3,8,32,128]{3,2,1,0:T(8,128)}, f32[8,32,128]{2,1,0:T(8,128)}, f32[16,1024]{1,0:T(8,128)}, f32[16,1024]{1,0:T(8,128)}, f32[4,384]{1,0:T(4,128)}, /*index=5*/f32[4,384]{1,0:T(4,128)}) custom-call(f32[3,8,32,128]{3,2,1,0:T(8,128)} %get-tuple-element.17.near_next, f32[8,32,128]{2,1,0:T(8,128)} %get-tuple-element.18.near_pressure, ...), custom_call_target="tpu_custom_call" | custom-call | tf_op jit(solution)/shard_map/emit/pallas_call | solution.py:896

commit v3 on v2

--- a/solution.py
+++ b/solution.py
@@ -636,16 +636,17 @@
     pltpu.VMEM((96, 384), BF16),
     pltpu.VMEM((4, 96, 384), BF16),
     pltpu.VMEM((4, 96, 384), BF16),
-    pltpu.VMEM((96, 1024), BF16),
-    pltpu.VMEM((4, 96, 1024), F32),
-    pltpu.VMEM((4, 96, 1024), BF16),
-    pltpu.VMEM((4, 96, 1024), BF16),
+    pltpu.VMEM((288, 1024), BF16),
+    pltpu.VMEM((96, 1024), F32),
+    pltpu.VMEM((384, 1024), F32),
+    pltpu.VMEM((384, 1024), BF16),
+    pltpu.VMEM((384, 1024), BF16),
     pltpu.VMEM((96, 384), F32),
     pltpu.VMEM((4, 96, 384), BF16),
     pltpu.VMEM((4, 96, 384), BF16),
-    pltpu.VMEM((4, 96, 1024), BF16),
-    pltpu.VMEM((4, 96, 1024), BF16),
-    pltpu.VMEM((96, 1024), BF16),
+    pltpu.VMEM((384, 1024), BF16),
+    pltpu.VMEM((384, 1024), BF16),
+    pltpu.VMEM((384, 1024), BF16),
     pltpu.VMEM((96, 1024), F32),
     pltpu.VMEM((1024, 384), BF16),
     pltpu.VMEM((4, 8, 384), F32),
@@ -674,7 +675,7 @@
     step = Stencil(here, velocity_next, pressure, refs[:n_stencil])
     refs = refs[n_stencil:]
     (
-        w_in, w_up, w_down, w_out, targets, in_all, err_all, lifted_b, slope, active, mixed,
+        w_in, w_up, w_down, w_out, targets, in_all, err_all, lifted_b, own_lift, slope, active, mixed,
         own_predicted, down_send, down_recv, back_raised, lift_b, back_b, own_back, w_in_t, tail_send, tail_recv,
         near_sems, in_sems, down_sems, err_sems, tail_sems,
     ) = refs[:N_TRAINER]
@@ -718,42 +719,58 @@
     make_fold(fold)
     for copy in near[:2]:
         copy.wait()
-    pick_patches(step.fields, selection, lines, fold, in_all.at[k])
+    pick_patches(step.fields, selection, lines, fold, in_all.at[0])
     step.prepare()
     greeted(met)
     step.send_one()
     in_copies = start(
-        [push(in_all.at[k], in_all.at[k], in_sems, d, peer(d)) for d in (2, 1, 3)]
+        [push(in_all.at[0], in_all.at[4 - d], in_sems, d, peer(d)) for d in (2, 1, 3)]
     )
     for copy in near[2:]:
         copy.wait()
 
-    def forward(owner, own):
-        rows = in_all[owner]
-        lifted = matmul(rows, w_in[...])
-        lifted_b[...] = lifted.astype(BF16)
+    def forward(first, count):
+        rows = in_all[first : first + count].reshape(96 * count, 384)
+        at_rows = slice(96 * first, 96 * (first + count))
+
+        def lift_in(n, carry):
+            at = columns(n)
+            lifted = matmul(rows, w_in[:, at])
+            lifted_b[0 : 96 * count, at] = lifted.astype(BF16)
+            if first == 0:
+                own_lift[:, at] = lifted
+            return carry
 
         def raise_(n, carry):
             at = columns(n)
-            raised = matmul(lifted_b[...], w_up[:, at])
+            raised = matmul(lifted_b[0 : 96 * count, :], w_up[:, at])
             sigmoid = jax.nn.sigmoid(raised)
-            active[owner, :, at] = (raised * sigmoid).astype(BF16)
-            slope[owner, :, at] = sigmoid * (1.0 + raised * (1.0 - sigmoid))
+            active[at_rows, at] = (raised * sigmoid).astype(BF16)
+            slope[at_rows, at] = sigmoid * (1.0 + raised * (1.0 - sigmoid))
             return carry
 
-        lax.fori_loop(0, 4, raise_, 0)
-        part = matmul(active[owner], w_down[...])
-        mixed[owner] = (lifted + part if own else part).astype(BF16)
-        return matmul(mixed[owner], w_out[...])
-
-    own_predicted[...] = forward(k, True)
+        def lower(n, carry):
+            at = columns(n)
+            part = matmul(active[at_rows, :], w_down[:, at])
+            if first == 0:
+                part = part + own_lift[:, at]
+            mixed[at_rows, at] = part.astype(BF16)
+            return carry
+
+        for body in (lift_in, raise_, lower):
+            lax.fori_loop(0, 4, body, 0)
+        return matmul(mixed[at_rows, :], w_out[...])
+
+    own_predicted[...] = forward(0, 1)
     w_in_t[...] = w_in[...].T
     step.make_source()
     step.send_two()
+    for copy in in_copies:
+        copy.wait_recv()
+    parts = forward(1, 3).astype(BF16)
     down_copies = []
-    for copy, d in zip(in_copies[1:] + in_copies[:1], (3, 1, 2)):
-        copy.wait_recv()
-        down_send[d] = forward(lax.rem(k + d, 4), False).astype(BF16)
+    for d in (2, 1, 3):
+        down_send[d] = parts[96 * (d - 1) : 96 * d]
         down_copies += start([push(down_send.at[d], down_recv.at[d], down_sems, d, peer(d))])
     step.solve()
     pick_patches(velocity_next, selection, lines, fold, targets)
@@ -764,49 +781,39 @@
     for d in (1, 2, 3):
         predicted = predicted + down_recv[d].astype(F32)
     scale = float(24576) ** (-0.5)
-    err_all[k] = ((predicted - targets[...].astype(F32)) * scale).astype(BF16)
+    err_all[0] = ((predicted - targets[...].astype(F32)) * scale).astype(BF16)
     err_copies = start(
-        [push(err_all.at[k], err_all.at[k], err_sems, d, peer(d)) for d in (2, 1, 3)]
+        [push(err_all.at[0], err_all.at[4 - d], err_sems, d, peer(d)) for d in (2, 1, 3)]
     )
-    def backward(owner, own):
-        errors = err_all[owner]
-
-        def back(n, carry):
-            at = columns(n)
-            both = matmul_nt(errors, w_out[at, :])
-            back_b[:, at] = both.astype(BF16)
-            if own:
-                own_back[:, at] = both
-            return carry
-
-        lax.fori_loop(0, 4, back, 0)
-
-        def back_up(n, carry):
-            at = columns(n)
-            steep = matmul_nt(back_b[...], w_down[at, :])
-            back_raised[owner, :, at] = (steep * slope[owner, :, at]).astype(BF16)
-            return carry
-
-        lax.fori_loop(0, 4, back_up, 0)
-
-    def lift(owner, own):
-        part = matmul_nt(back_raised[owner], w_up[...])
-        lift_b[owner] = (part + own_back[...] if own else part).astype(BF16)
-
-    backward(k, True)
-    lift(k, True)
-    for copy, d in zip(err_copies[1:], (3, 1)):
+    for copy in err_copies:
         copy.wait_recv()
-        owner = lax.rem(k + d, 4)
-        backward(owner, False)
-        lift(owner, False)
-    err_copies[0].wait_recv()
-    owner = lax.rem(k + 2, 4)
-    backward(owner, False)
     rows_in = in_all[...].reshape(384, 384)
     errors = err_all[...].reshape(384, 384)
-    up.fill(back_raised.reshape(384, 1024), rows_in)
-    down.fill(active.reshape(384, 1024), errors)
+
+    def back(n, carry):
+        at = columns(n)
+        both = matmul_nt(errors, w_out[at, :])
+        back_b[:, at] = both.astype(BF16)
+        own_back[:, at] = both[0:96]
+        return carry
+
+    def back_up(n, carry):
+        at = columns(n)
+        steep = matmul_nt(back_b[...], w_down[at, :])
+        back_raised[:, at] = (steep * slope[:, at]).astype(BF16)
+        return carry
+
+    def back_lift(n, carry):
+        at = columns(n)
+        part = matmul_nt(back_raised[...], w_up[at, :])
+        lift_b[0:96, at] = (part[0:96] + own_back[:, at]).astype(BF16)
+        lift_b[96:384, at] = part[96:384].astype(BF16)
+        return carry
+
+    lax.fori_loop(0, 4, back, 0)
+    lax.fori_loop(0, 4, back_up, 0)
+    up.fill(back_raised, rows_in)
+    down.fill(active, errors)
 
     def grad_chunk(scatter, left, right):
         def chunk(n, carry):
@@ -819,11 +826,11 @@
 
         lax.fori_loop(0, 4, chunk, 0)
 
-    lift(owner, False)
     up.first()
-    grad_chunk(grad_in, lift_b.reshape(384, 1024), rows_in)
+    lax.fori_loop(0, 4, back_lift, 0)
+    grad_chunk(grad_in, lift_b, rows_in)
     down.first()
-    grad_chunk(grad_out, mixed.reshape(384, 1024), errors)
+    grad_chunk(grad_out, mixed, errors)
     scatters = (grad_in, grad_out)
     for scatter in scatters:
         scatter.first(0)

time: 91.3 us -> 86.6 us (0.949)
  Pallas kernels: 90 us -> 84.4 us
    pallas_call x1, Pallas kernels: 88.1 us -> 82.5 us  [on_device(): pl.pallas_call(step_kernel, out_shape=[shape((3, 8, 32, 128), F32), shape...]
where the time goes in v3:
time: 86.6 us; the launch traced here: 85.1 us
  Pallas kernels  84.4 us (97%)
    pallas_call x1, Pallas kernels, on_device(): pl.pallas_call(step_kernel, out_shape=[shape((3, 8, 32, 128), F32), shape...  82.5 us
    pallas_call x1, Pallas kernels, on_device(): pl.pallas_call(emit_kernel, out_shape=[shape((3, 8, 32, 128), F32), shape...  1.95 us

profile of v3, /device:TPU:32, one launch (start us, length us, event | category | flops | bytes accessed | tf_op | source)
XLA Modules:
  0.0 85.1 jit_solution(483831469762009013)
XLA Ops:
  0.6 82.5 %step.1 = (f32[3,8,32,128]{3,2,1,0:T(8,128)}, f32[8,32,128]{2,1,0:T(8,128)}, f32[16,1024]{1,0:T(8,128)}, f32[16,1024]{1,0:T(8,128)}, f32[8,384]{1,0:T(8,128)}) custom-call(f32[3,8,32,128]{3,2,1,0:T(8,128)} %velocity.1, f32[8,32,128]{2,1,0:T(8,128)} %viscosity.1, s32[1,96]{1,0:T(1,128)} %bitcast.3, bf16[384,1024]{1,0:T(8,128)(2,1)} %w_in_far.1, ...), custom_call_target="tpu_custom_call" | custom-call | tf_op jit(solution)/shard_map/step/pallas_call | solution.py:886
  83.1 1.9 %emit.1 = (f32[3,8,32,128]{3,2,1,0:T(8,128)}, f32[8,32,128]{2,1,0:T(8,128)}, f32[16,1024]{1,0:T(8,128)}, f32[16,1024]{1,0:T(8,128)}, f32[4,384]{1,0:T(4,128)}, /*index=5*/f32[4,384]{1,0:T(4,128)}) custom-call(f32[3,8,32,128]{3,2,1,0:T(8,128)} %get-tuple-element.17.near_next, f32[8,32,128]{2,1,0:T(8,128)} %get-tuple-element.18.near_pressure, ...), custom_call_target="tpu_custom_call" | custom-call | tf_op jit(solution)/shard_map/emit/pallas_call | solution.py:903

commit v4 on v3

--- a/solution.py
+++ b/solution.py
@@ -310,7 +310,11 @@
                     new[t, x, 8:56, :] = (total - swide[t, x]) * scale[t]
                 return carry
 
-            lax.fori_loop(sweep, 20 - sweep, relax, 0)
+            def pair(n, carry, relax=relax, sweep=sweep):
+                relax(sweep + 2 * n, carry)
+                return relax(sweep + 2 * n + 1, carry)
+
+            lax.fori_loop(0, 10 - sweep, pair, 0)
             old, new = new, old
         p, prov = old, self.prov
 
@@ -757,8 +761,9 @@
             mixed[at_rows, at] = part.astype(BF16)
             return carry
 
-        for body in (lift_in, raise_, lower):
-            lax.fori_loop(0, 4, body, 0)
+        lax.fori_loop(0, 4, lift_in, 0)
+        for body in (raise_, lower):
+            lax.fori_loop(0, 4, body, 0, unroll=True)
         return matmul(mixed[at_rows, :], w_out[...])
 
     own_predicted[...] = forward(0, 1)
@@ -811,7 +816,7 @@
         return carry
 
     lax.fori_loop(0, 4, back, 0)
-    lax.fori_loop(0, 4, back_up, 0)
+    lax.fori_loop(0, 4, back_up, 0, unroll=True)
     up.fill(back_raised, rows_in)
     down.fill(active, errors)
 

time: 86.6 us -> 85.1 us (0.983)
  no operation moved by 1% of the time
where the time goes in v4:
time: 85.1 us; the launch traced here: 84.2 us
  Pallas kernels  83.6 us (98%)
    pallas_call x1, Pallas kernels, on_device(): pl.pallas_call(step_kernel, out_shape=[shape((3, 8, 32, 128), F32), shape...  81.7 us
    pallas_call x1, Pallas kernels, on_device(): pl.pallas_call(emit_kernel, out_shape=[shape((3, 8, 32, 128), F32), shape...  1.95 us

profile of v4, /device:TPU:32, one launch (start us, length us, event | category | flops | bytes accessed | tf_op | source)
XLA Modules:
  0.0 84.2 jit_solution(5961831705707348987)
XLA Ops:
  0.6 81.7 %step.1 = (f32[3,8,32,128]{3,2,1,0:T(8,128)}, f32[8,32,128]{2,1,0:T(8,128)}, f32[16,1024]{1,0:T(8,128)}, f32[16,1024]{1,0:T(8,128)}, f32[8,384]{1,0:T(8,128)}) custom-call(f32[3,8,32,128]{3,2,1,0:T(8,128)} %velocity.1, f32[8,32,128]{2,1,0:T(8,128)} %viscosity.1, s32[1,96]{1,0:T(1,128)} %bitcast.3, bf16[384,1024]{1,0:T(8,128)(2,1)} %w_in_far.1, ...), custom_call_target="tpu_custom_call" | custom-call | tf_op jit(solution)/shard_map/step/pallas_call | solution.py:891
  82.3 1.9 %emit.1 = (f32[3,8,32,128]{3,2,1,0:T(8,128)}, f32[8,32,128]{2,1,0:T(8,128)}, f32[16,1024]{1,0:T(8,128)}, f32[16,1024]{1,0:T(8,128)}, f32[4,384]{1,0:T(4,128)}, /*index=5*/f32[4,384]{1,0:T(4,128)}) custom-call(f32[3,8,32,128]{3,2,1,0:T(8,128)} %get-tuple-element.17.near_next, f32[8,32,128]{2,1,0:T(8,128)} %get-tuple-element.18.near_pressure, ...), custom_call_target="tpu_custom_call" | custom-call | tf_op jit(solution)/shard_map/emit/pallas_call | solution.py:908
